TPU v7x, 256 devices: a whole 4x4x8 slice. The times are simulated.
256 devices in a mesh: row: 64 (over y, z, core), cand: 4 (over x).
Axes of the slice: x: 4, y: 4, z: 8, core: 2. Of those that a mesh axis runs over, the one named last changes fastest.
Arguments:
- cross_cov: float32 [65536, 4096], P('row', 'cand'), may hold values from -3 to 3
- factor_cols: float32 [65536, 1024], P('row'), as said below
- prior_cov: float32 [4096, 4096], P('row', 'cand'), may hold values from -6 to 6
Outputs:
- solved_rhs: float32 [65536, 4096], P('row', 'cand')
- posterior_cov: float32 [4096, 4096], P('row', 'cand')
Inputs may be any that keep to these rules, and one draw needn't show every extreme that they name: In block s, the entries of factor_cols at row s * 1024 + i and column s * 256 + i (the diagonal of D_s) lie between 1 and 2.
All inputs are finite; a program needn't handle non-finite values.
Results may differ from a plain program's by a relative error of at most 0.0001.
Values sent between devices are 32-bit elements; how exact they have to be, the bound alone decides.
A program may use at most 128 MiB of HBM per device.

v0:
```python
import jax
import jax.numpy as jnp
from jax import lax
from jax.sharding import PartitionSpec as P

PANEL = 256
STEPS = 4


def broadcast(x, axis, root):
    mine = lax.axis_index(axis) == root
    return lax.psum(jnp.where(mine, x, jnp.zeros_like(x)), axis)


def lower_product(left_side, right_side):
    return lax.dot_general(
        left_side,
        right_side,
        (((0,), (0,)), ((), ())),
        precision=lax.Precision.HIGHEST,
        preferred_element_type=jnp.float32,
    )


def solve_lower(diagonal, values):
    return lax.linalg.triangular_solve(diagonal, values, left_side=True, lower=True)


def local(cross_cov, factor_cols, prior_cov):
    highest_precision = lax.Precision.HIGHEST
    row_count = cross_cov.shape[0]
    columns = cross_cov.shape[1]
    sig_rows = prior_cov.shape[0]
    row_index = lax.axis_index("row")
    offset = row_index * sig_rows % columns
    holder = row_index * sig_rows // columns
    position = lax.broadcasted_iota(jnp.int32, (row_count, 1), 0)
    leading = position < PANEL
    solutions = []
    current = cross_cov
    for section in range(STEPS):
        factor_block = factor_cols[:, section * PANEL : (section + 1) * PANEL]
        own_solution = solve_lower(factor_block[:PANEL], current[:PANEL])
        solution = broadcast(own_solution, "row", section)
        update = jnp.dot(
            factor_block, solution, precision=highest_precision, preferred_element_type=jnp.float32
        )
        finished = leading & (row_index <= section)
        current = jnp.where(finished, current, current - update)
        current = current.at[:PANEL].set(jnp.where(row_index == section, solution, current[:PANEL]))
        solutions.append(solution)
    posterior = prior_cov
    for solution in solutions:
        columns_part = lax.dynamic_slice_in_dim(solution, offset, sig_rows, 1)
        posterior = posterior - lower_product(broadcast(columns_part, "cand", holder), solution)
    return (current, posterior)


def solution(mesh):
    placed = (P("row", "cand"), P("row", None), P("row", "cand"))
    return jax.shard_map(
        local,
        mesh=mesh,
        in_specs=placed,
        out_specs=(P("row", "cand"), P("row", "cand")),
        check_vma=False,
    )
```

profile of v0, /device:TPU:1, one launch (start us, length us, event | category | flops | bytes accessed | tf_op | source)
XLA Modules:
  0.0 879.2 jit_solution(8052604530371672772)
XLA Ops:
  8.6 4.0 while.12
  12.6 19.7 %custom-call.6 = f32[2,128,128]{1,2,0:T(8,128)S(1)} custom-call(f32[2,128,128]{2,1,0:T(8,128)S(1)} %get-tuple-element.77), custom_call_target="InvertDiagBlocksLowerTriangular" | custom-call | tf_op jit(solution)/shard_map/triangular_solve/custom-call.1 | solution.py:26
  37.6 3.8 while.13
  41.4 19.7 %custom-call.7 = f32[2,128,128]{1,2,0:T(8,128)S(1)} custom-call(f32[2,128,128]{2,1,0:T(8,128)S(1)} %get-tuple-element.78), custom_call_target="InvertDiagBlocksLowerTriangular" | custom-call | tf_op jit(solution)/shard_map/triangular_solve/custom-call.1 | solution.py:26
  61.1 164.2 %all-reduce.7.cloned.1.call-done = f32[256,1024]{1,0:T(8,128)} async-done(((f32[256,1024]{1,0:T(8,128)}), f32[256,1024]{1,0:T(8,128)}) %all-reduce.7.cloned.1.call-update) | async-done | bytes 1048592 | tf_op jit(solution)/shard_map/psum | solution.py:12
  225.3 8.6 subtract_select_fusion.3
  233.9 2.4 constant_dynamic-update-slice_fusion.2
  239.5 4.0 while.14
  243.5 19.7 %custom-call.8 = f32[2,128,128]{1,2,0:T(8,128)S(1)} custom-call(f32[2,128,128]{2,1,0:T(8,128)S(1)} %get-tuple-element.79), custom_call_target="InvertDiagBlocksLowerTriangular" | custom-call | tf_op jit(solution)/shard_map/triangular_solve/custom-call.1 | solution.py:26
  263.2 159.7 %all-reduce.9.cloned.1.call-done = f32[256,1024]{1,0:T(8,128)} async-done(((f32[256,1024]{1,0:T(8,128)}), f32[256,1024]{1,0:T(8,128)}) %all-reduce.9.cloned.1.call-update) | async-done | bytes 1048592 | tf_op jit(solution)/shard_map/psum | solution.py:12
  422.9 8.6 subtract_select_fusion.2
  431.5 2.3 constant_dynamic-update-slice_fusion.1
  437.1 4.0 while.15
  441.1 19.7 %custom-call.9 = f32[2,128,128]{1,2,0:T(8,128)S(1)} custom-call(f32[2,128,128]{2,1,0:T(8,128)S(1)} %get-tuple-element.80), custom_call_target="InvertDiagBlocksLowerTriangular" | custom-call | tf_op jit(solution)/shard_map/triangular_solve/custom-call.1 | solution.py:26
  460.8 159.2 %all-reduce.11.cloned.1.call-done = f32[256,1024]{1,0:T(8,128)} async-done(((f32[256,1024]{1,0:T(8,128)}), f32[256,1024]{1,0:T(8,128)}) %all-reduce.11.cloned.1.call-update) | async-done | bytes 1048592 | tf_op jit(solution)/shard_map/psum | solution.py:12
  619.9 8.6 subtract_select_fusion.1
  628.5 2.3 constant_dynamic-update-slice_fusion
  636.5 180.9 %all-reduce.13.cloned.1.call-done = f32[256,1024]{1,0:T(8,128)} async-done(((f32[256,1024]{1,0:T(8,128)}), f32[256,1024]{1,0:T(8,128)}) %all-reduce.13.cloned.1.call-update) | async-done | bytes 1048592 | tf_op jit(solution)/shard_map/psum | solution.py:12
  819.1 8.6 subtract_select_fusion
  827.8 2.4 fusion
  830.1 35.9 %all-reduce.15.cloned.1.call-done = (f32[256,64]{1,0:T(8,128)}, f32[256,64]{1,0:T(8,128)}, f32[256,64]{1,0:T(8,128)}, f32[256,64]{1,0:T(8,128)}) async-done(((f32[256,64]{1,0:T(8,128)}, f32[256,64]{1,0:T(8,128)}, f32[256,64]{1,0:T(8,128)}, f32[256,64]{1,0:T(8,128)}), (f32[256,64]{1,0:T(8,128)}, f32[256,64]{1,0:T(8,128)}, f32[256,64]{1,0:T(8,128)}, f32[256,64]{1,0:T(8,128)})) %all-reduce.15.cloned.1.call-update) | async-done | bytes 262160 | tf_op jit(solution)/shard_map/psum | solution.py:12
  866.1 1.8 convolution_subtract_fusion.7
  867.8 1.7 convolution_subtract_fusion.6
  869.5 1.7 convolution_subtract_fusion.5
  (80 shorter events, 37.3 us)
Async XLA Ops:
  7.2 218.1 %all-reduce.7.cloned.1.call-start = ((), (), s32[]{:S(2)}) async-start(), calls=%async_computation | async-start | bytes 2097152 | tf_op jit(solution)/shard_map/psum | solution.py:12
  37.3 385.5 %all-reduce.9.cloned.1.call-start = ((), (), s32[]{:S(2)}) async-start(), calls=%async_computation.1 | async-start | bytes 2097152 | tf_op jit(solution)/shard_map/psum | solution.py:12
  225.3 8.6 copy-start
  239.3 380.7 %all-reduce.11.cloned.1.call-start = ((), (), s32[]{:S(2)}) async-start(), calls=%async_computation.2 | async-start | bytes 2097152 | tf_op jit(solution)/shard_map/psum | solution.py:12
  422.9 8.6 copy-start.1
  436.8 380.7 %all-reduce.13.cloned.1.call-start = ((), (), s32[]{:S(2)}) async-start(), calls=%async_computation.3 | async-start | bytes 2097152 | tf_op jit(solution)/shard_map/psum | solution.py:12
  619.9 8.6 copy-start.2
  633.8 232.2 %all-reduce.15.cloned.1.call-start = ((), (), s32[]{:S(2)}) async-start(), calls=%async_computation.4 | async-start | bytes 1048576 | tf_op jit(solution)/shard_map/psum | solution.py:12
  819.1 8.7 copy-start.3
  819.1 46.9 %copy-start.5 = (f32[64,1024]{1,0:T(8,128)S(1)}, f32[64,1024]{1,0:T(8,128)}, u32[]{:S(2)}) copy-start(f32[64,1024]{1,0:T(8,128)} %param.15) | copy-start | bytes 786436
  866.1 5.1 copy-start.4
  866.1 5.1 copy-start.6
Sparse Core Ops, SparseCore 0:
  37.4 187.7 all-reduce.6
  239.4 183.4 all-reduce.8
  436.9 182.9 all-reduce.10
  634.0 183.4 all-reduce.12
  820.4 45.6 all-reduce.14
where the time goes:
time: 881 us; the launch traced here: 879 us
  waiting for transfers between devices  700 us (79%)
  other arithmetic  97.6 us (11%)
  matrix products  50.5 us (6%)
  local copies, waits for them, and re-layouts  15.6 us (2%)
  between operations  14.1 us (2%)
    psum x5, waiting for transfers between devices, broadcast(): return lax.psum(jnp.where(mine, x, jnp.zeros_like(x)), axis)  700 us
    another operation x6, other arithmetic, solve_lower(): lax.linalg.triangular_solve(diagonal, values, left_side=True, lower=True)  80 us
    dot_general x4, matrix products, local(): jnp.dot(factor_block, solution, precision=highest_precision, preferred_el...  34.5 us
  transfers between devices with their start and end apart: 5, of which 5 were waited for; matrix products, arithmetic and copies ran while one was open for 10% of the time, Pallas kernels for 0%

commit v1 on v0

v1 whole, which is shorter than its diff:
```python
import functools

import jax
import jax.numpy as jnp
from jax import lax
from jax.experimental import pallas as pl
from jax.experimental.pallas import tpu as pltpu
from jax.sharding import PartitionSpec as P

MESH = pl.DeviceIdType.MESH
F32, BF16 = jnp.float32, jnp.bfloat16
HIGHEST = lax.Precision.HIGHEST
B = 256
SUB = 1
PIECE = 64 // SUB
LAG = 2
DPOS = 1

TREES = (
    (2, 112, 98, 82, 74, 62, 46, 22, 48, 96, 112, 98, 86, 66, 48, 37, 65, 93, 96, 112, 98, 81, 96, 49, 80, 96, 112, 98, 82, 72, 49, 65),
    (1, 21, 45, 61, 69, 81, 97, 112, 48, 38, 48, 64, 81, 97, 112, 96, 66, 50, 96, 82, 97, 112, 96, 94, 80, 66, 50, 73, 89, 97, 112, 96),
    (8, 48, 64, 80, 96, 80, 64, 48, 48, 96, 82, 96, 112, 96, 81, 96, 40, 48, 73, 88, 104, 90, 74, 48, 27, 45, 61, 68, 84, 70, 62, 46),
    (4, 56, 64, 80, 96, 80, 64, 56, 23, 41, 61, 77, 88, 76, 62, 42, 36, 80, 70, 85, 100, 84, 69, 80, 48, 64, 80, 96, 112, 96, 80, 64),
)
STEP = ((0, 1), (0, 7), (1, 0), (3, 0))
FIRST = (1, 0, 3, 2)
NL = (1, 5)
NB = (11, 15)
BASE = (0, 11)
BLOCKS = 26
LOWER = (((1, 0),), ((3, 2), (2, 0), (3, 0), (2, 1), (3, 1)))
DEPTH = 7
UNITS = NB[1] * SUB + LAG * DEPTH


def b_index(q, s):
    rho, half = s // 2, s % 2
    return BASE[rho] + NL[rho] + 2 * q + half + jnp.where(q >= DPOS, 2, 0)


def d_index(s):
    rho, half = s // 2, s % 2
    return BASE[rho] + NL[rho] + 2 * DPOS + half


def l_index(s, t):
    rho = s // 2
    return BASE[rho] + LOWER[rho].index((s, t))


def split(x):
    hi = x.astype(BF16)
    return hi, (x - hi.astype(F32)).astype(BF16)


def dot(a, b):
    return jnp.dot(a, b, preferred_element_type=F32)


def dot3(ah, al, bh, bl):
    return dot(ah, bh) + (dot(ah, bl) + dot(al, bh))


def dotf(a, b):
    return jnp.dot(a, b, precision=HIGHEST, preferred_element_type=F32)


def invert_lower(d):
    ri = lax.broadcasted_iota(jnp.int32, (B, B), 0)
    ci = lax.broadcasted_iota(jnp.int32, (B, B), 1)
    same = ri == ci
    on_diag = jnp.where(same, d, 0.0)
    by_row = 1.0 / jnp.sum(on_diag, axis=1, keepdims=True)
    by_col = 1.0 / jnp.sum(on_diag, axis=0, keepdims=True)
    n = jnp.where(ri > ci, d, 0.0) * by_row
    inv = jnp.where(same, 1.0, 0.0) - jnp.where((ri >> 1) == (ci >> 1), n, 0.0)
    for k in range(1, 8):
        off = jnp.where(((ri >> (k + 1)) == (ci >> (k + 1))) & ((ri >> k) != (ci >> k)), n, 0.0)
        inv = inv - dotf(dotf(inv, off), inv)
    return inv * by_col


def kernel(
    c_hbm, f_hbm, p_hbm, out_hbm, post_hbm,
    w, fv, fh, fl, cv, pv, xh, xl, lh, ll, dv, xb, sbt, tv,
    rs, sb, child_sem, sib_sem, own_sem, load_sem, raw_sem, out_sem, xr, xs, xsb, xss,
):
    row = lax.axis_index("row")
    x = lax.axis_index("cand")
    y = row // 16
    z = (row // 2) % 8
    core = row % 2

    def device(yy, zz, cc, xx=None):
        return ((yy % 4) * 16 + (zz % 8) * 2 + cc, x if xx is None else xx % 4)

    sibling = device(y, z, 1 - core)

    def towards(d, cc):
        return device(y + STEP[d][0], z + STEP[d][1], cc)

    load_f = pltpu.make_async_copy(f_hbm, fv, load_sem.at[0])
    load_c = pltpu.make_async_copy(c_hbm, cv, load_sem.at[1])
    load_p = pltpu.make_async_copy(p_hbm, pv, load_sem.at[2])

    def raw_blocks(s):
        found = []
        for t in range(s):
            found.append((l_index(s, t), f_hbm.at[pl.ds(0, B), pl.ds(t * B, B)]))
        for q in range(4):
            b = BASE[s // 2] + NL[s // 2] + 2 * q + s % 2 + (2 if q >= DPOS else 0)
            found.append((b, c_hbm.at[pl.ds(0, B), pl.ds(q * B, B)]))
        return sorted(found, key=lambda e: e[0])

    for s in range(4):

        @pl.when(row == s)
        def _(s=s):
            pltpu.make_async_copy(f_hbm.at[pl.ds(0, B), pl.ds(s * B, B)], dv, raw_sem.at[7]).start()
            for i, (b, src) in enumerate(raw_blocks(s)):
                pltpu.make_async_copy(src, w.at[b], raw_sem.at[i]).start()

    barrier = pltpu.get_barrier_semaphore()
    for d in range(4):
        for cc in range(2):
            pl.semaphore_signal(barrier, inc=1, device_id=towards(d, cc), device_id_type=MESH)
    for dx in (1, 3):
        pl.semaphore_signal(barrier, inc=1, device_id=device(y, z, core, x + dx), device_id_type=MESH)
    pl.semaphore_signal(barrier, inc=1, device_id=sibling, device_id_type=MESH)
    load_f.start()
    load_c.start()
    load_p.start()
    pl.semaphore_wait(barrier, 11)

    def own_copies(s, b, slot):
        copies = []
        for tree in range(4):
            for k in range(SUB):
                rows = w.at[b, pl.ds(64 * tree + PIECE * k, PIECE)]
                for other in range(2):
                    if other:
                        sem = (rs if tree // 2 != s % 2 else sb).at[b * SUB + k, tree % 2]
                        to = sibling
                    else:
                        sem = rs.at[b * SUB + k, tree % 2]
                        to = towards(FIRST[tree], tree // 2)
                    copies.append(
                        pltpu.make_async_remote_copy(
                            src_ref=rows, dst_ref=rows, send_sem=own_sem.at[slot, (tree * SUB + k) * 2 + other],
                            recv_sem=sem, device_id=to, device_id_type=MESH,
                        )
                    )
        return copies

    def own_blocks(s):
        found = [b for b, _ in raw_blocks(s)]
        return found

    for s in range(4):

        @pl.when(row == s)
        def _(s=s):
            d_block = BASE[s // 2] + NL[s // 2] + 2 * DPOS + s % 2
            blocks = raw_blocks(s)
            done = False
            for i, (b, src) in enumerate(blocks):
                pltpu.make_async_copy(src, w.at[b], raw_sem.at[i]).wait()
            first = [i for i, (b, _) in enumerate(blocks) if b < d_block]
            later = [i for i, (b, _) in enumerate(blocks) if b > d_block]
            for i in first:
                for c in own_copies(s, blocks[i][0], i):
                    c.start()
            pltpu.make_async_copy(f_hbm.at[pl.ds(0, B), pl.ds(s * B, B)], dv, raw_sem.at[7]).wait()
            w[d_block] = invert_lower(dv[...])
            for c in own_copies(s, d_block, 7):
                c.start()
            for i in later:
                for c in own_copies(s, blocks[i][0], i):
                    c.start()

    load_f.wait()

    @pl.loop(0, 16)
    def _(i):
        rows = pl.ds(pl.multiple_of(i * 64, 64), 64)
        hi, lo = split(fv[rows, :])
        fh[rows, :] = hi
        fl[rows, :] = lo

    def lookup(table, key):
        found = jnp.int32(0)
        for k, v in enumerate(table):
            found = jnp.where(key == k, v, found)
        return found

    place = []
    for rho in range(2):
        idx = y * 8 + (z - rho + 8) % 8
        merged = [TREES[2 * cc][k] + 128 * TREES[2 * cc + 1][k] for cc in range(2) for k in range(32)]
        v = lookup(merged, core * 32 + idx)
        place.append((idx == 0, (v % 128, v // 128)))

    def piece(b, k, rows_tree):
        return w.at[b, pl.ds(pl.multiple_of(rows_tree * 64 + k * PIECE, 8), PIECE)]

    def forward(rho, il, n):
        is_root, values = place[rho]
        mask = values[il] % 16
        block_n = n // SUB
        b = BASE[rho] + block_n
        k = n % SUB
        ref = piece(b, k, 2 * core + il)
        sem_i = b * SUB + k

        @pl.when(jnp.logical_or(jnp.logical_not(is_root), (block_n + 1) % 2 != core))
        def _():
            pltpu.make_async_remote_copy(
                src_ref=ref, dst_ref=ref, send_sem=sib_sem.at[rho, il], recv_sem=rs.at[sem_i, il],
                device_id=sibling, device_id_type=MESH,
            ).wait_recv()

        @pl.when(jnp.logical_not(is_root))
        def _():
            for d in range(4):

                @pl.when((mask // 2**d) % 2 == 1)
                def _(d=d):
                    pltpu.make_async_remote_copy(
                        src_ref=ref, dst_ref=ref, send_sem=child_sem.at[rho, il, d], recv_sem=rs.at[sem_i, il],
                        device_id=towards(d, core), device_id_type=MESH,
                    ).start()

            pltpu.make_async_remote_copy(
                src_ref=ref, dst_ref=ref, send_sem=sib_sem.at[rho, il], recv_sem=sb.at[sem_i, il],
                device_id=sibling, device_id_type=MESH,
            ).start()

    def step(u, carry):
        for rho in range(2):
            for il in range(2):
                n = u - LAG * (place[rho][1][il] // 16)

                @pl.when(jnp.logical_and(n >= 0, n < NB[rho] * SUB))
                def _(rho=rho, il=il, n=n):
                    forward(rho, il, n)

        return carry

    lax.fori_loop(0, UNITS, step, 0)

    p = (x - y + 4) % 4
    qz = z // 2
    half = pl.ds(pl.multiple_of(core * 128, 128), 128)
    lanes = pl.ds(pl.multiple_of((z % 2) * 128, 128), 128)

    def x_copy(s, dx, src, slot):
        return pltpu.make_async_remote_copy(
            src_ref=src, dst_ref=xb.at[s, half], send_sem=xs.at[slot, s], recv_sem=xr.at[s],
            device_id=device(y, z, core, x + dx), device_id_type=MESH,
        )

    def x_sibling(s):
        return pltpu.make_async_remote_copy(
            src_ref=xb.at[s, half], dst_ref=xb.at[s, half], send_sem=xss.at[s], recv_sem=xsb.at[s],
            device_id=sibling, device_id_type=MESH,
        )

    def x_source(s):
        return w.at[b_index(qz, s), half, lanes]

    @pl.when(p == 0)
    def _():
        for s in range(4):
            x_copy(s, 1, x_source(s), 0).start()
            x_copy(s, 3, x_source(s), 1).start()

    relays = jnp.logical_or(jnp.logical_and(p == 1, core == 0), jnp.logical_and(p == 3, core == 1))
    onward = jnp.where(core == 0, 1, 3)

    def x_relay():
        for s in range(4):
            x_copy(s, 1, x_source(s), 0).wait_recv()

            @pl.when(relays)
            def _(s=s):
                x_copy(s, onward, xb.at[s, half], 0).start()

            x_sibling(s).start()

    def wait_other(b, rho, block_n):
        is_root = place[rho][0]

        @pl.when(jnp.logical_or(jnp.logical_not(is_root), (block_n + 1) % 2 != core))
        def _():
            for il in range(2):
                for k in range(SUB):
                    ref = piece(b, k, 2 * (1 - core) + il)
                    pltpu.make_async_remote_copy(
                        src_ref=ref, dst_ref=ref, send_sem=sib_sem.at[rho, il], recv_sem=sb.at[b * SUB + k, il],
                        device_id=sibling, device_id_type=MESH,
                    ).wait_recv()

    for s in range(4):
        for t in range(s):
            b = l_index(s, t)
            wait_other(b, s // 2, b - BASE[s // 2])
            hi, lo = split(w[b])
            lh[s * (s - 1) // 2 + t] = hi
            ll[s * (s - 1) // 2 + t] = lo
        b = BASE[s // 2] + NL[s // 2] + 2 * DPOS + s % 2
        wait_other(b, s // 2, b - BASE[s // 2])
        hi, lo = split(w[b])
        lh[6 + s] = hi
        ll[6 + s] = lo

    def solve(load, store):
        parts = []
        for s in range(4):
            r = load(s)
            for t in range(s):
                i = s * (s - 1) // 2 + t
                r = r - dot3(lh[i], ll[i], *parts[t])
            v = dot3(lh[6 + s], ll[6 + s], *split(r))
            parts.append(split(v))
            store(s, v, *parts[s])

    load_c.wait()

    def group(q):
        cols = pl.ds(pl.multiple_of(q * B, B), B)
        for s in range(4):
            b = b_index(q, s)
            wait_other(b, s // 2, b - BASE[s // 2])

        def store(s, v, hi, lo):
            xh[pl.ds(s * B, B), cols] = hi
            xl[pl.ds(s * B, B), cols] = lo

            @pl.when(row == s)
            def _():
                dv[...] = v

        solve(lambda s: w[b_index(q, s)], store)
        for m in range(4):
            rows = pl.ds(m * B, B)
            cv[rows, cols] = cv[rows, cols] - dot3(fh[rows, :], fl[rows, :], xh[:, cols], xl[:, cols])

        @pl.when(row < 4)
        def _():
            cv[pl.ds(0, B), cols] = dv[...]

        pltpu.make_async_copy(cv.at[:, cols], out_hbm.at[:, cols], out_sem.at[q]).start()

    @pl.loop(0, 4)
    def _(q):
        group(q)

        @pl.when(jnp.logical_and(q == 1, jnp.logical_or(p == 1, p == 3)))
        def _():
            x_relay()

        @pl.when(jnp.logical_and(q == 2, p == 2))
        def _():
            x_relay()

    @pl.when(p == 0)
    def _():
        for s in range(4):
            xb[s] = w[b_index(qz, s), :, lanes]

    @pl.when(p != 0)
    def _():
        for s in range(4):
            other = xb.at[s, pl.ds(pl.multiple_of((1 - core) * 128, 128), 128)]
            pltpu.make_async_remote_copy(
                src_ref=other, dst_ref=other, send_sem=xss.at[s], recv_sem=xsb.at[s],
                device_id=sibling, device_id_type=MESH,
            ).wait_recv()

    def store_t(s, v, hi, lo):
        sbt[:, pl.ds(s * B, B)] = v.T

    solve(lambda s: xb[s], store_t)
    load_p.wait()
    sh, sl = split(sbt[pl.ds(pl.multiple_of(core * 64, 64), 64), :])

    for q in range(4):
        cols = pl.ds(q * B, B)
        tv[:, cols] = pv[:, cols] - dot3(sh, sl, xh[:, cols], xl[:, cols])

    save_p = pltpu.make_async_copy(tv, post_hbm, out_sem.at[4])
    save_p.start()

    for s in range(4):

        @pl.when(row == s)
        def _(s=s):
            for i, (b, _) in enumerate(raw_blocks(s)):
                for c in own_copies(s, b, i):
                    c.wait_send()
            for c in own_copies(s, BASE[s // 2] + NL[s // 2] + 2 * DPOS + s % 2, 7):
                c.wait_send()

    for rho in range(2):
        is_root, values = place[rho]
        whole = w.at[pl.ds(0, NB[rho]), pl.ds(0, 64)]

        @pl.when(jnp.logical_not(is_root))
        def _(rho=rho, values=values, whole=whole):
            for il in range(2):
                for d in range(4):

                    @pl.when((values[il] % 16 // 2**d) % 2 == 1)
                    def _(il=il, d=d):
                        pltpu.make_async_remote_copy(
                            src_ref=whole, dst_ref=whole, send_sem=child_sem.at[rho, il, d], recv_sem=rs.at[0, il],
                            device_id=towards(d, core), device_id_type=MESH,
                        ).wait_send()

                pltpu.make_async_remote_copy(
                    src_ref=whole, dst_ref=whole, send_sem=sib_sem.at[rho, il], recv_sem=rs.at[0, il],
                    device_id=sibling, device_id_type=MESH,
                ).wait_send()

    @pl.when(p == 0)
    def _():
        for s in range(4):
            x_copy(s, 1, x_source(s), 0).wait_send()
            x_copy(s, 3, x_source(s), 1).wait_send()

    @pl.when(p != 0)
    def _():
        for s in range(4):

            @pl.when(relays)
            def _(s=s):
                x_copy(s, onward, xb.at[s, half], 0).wait_send()

            x_sibling(s).wait_send()

    save_p.wait()
    for q in range(4):
        cols = pl.ds(q * B, B)
        pltpu.make_async_copy(cv.at[:, cols], out_hbm.at[:, cols], out_sem.at[q]).wait()


def local(cross_cov, factor_cols, prior_cov):
    n = 1024
    dma = pltpu.SemaphoreType.DMA
    any_space = pl.BlockSpec(memory_space=pl.ANY)
    return pl.pallas_call(
        kernel,
        out_shape=(jax.ShapeDtypeStruct((n, n), F32), jax.ShapeDtypeStruct((64, n), F32)),
        in_specs=[any_space] * 3,
        out_specs=(any_space, any_space),
        scratch_shapes=[
            pltpu.VMEM((BLOCKS, B, B), F32),
            pltpu.VMEM((n, n), F32),
            pltpu.VMEM((n, n), BF16),
            pltpu.VMEM((n, n), BF16),
            pltpu.VMEM((n, n), F32),
            pltpu.VMEM((64, n), F32),
            pltpu.VMEM((n, n), BF16),
            pltpu.VMEM((n, n), BF16),
            pltpu.VMEM((10, B, B), BF16),
            pltpu.VMEM((10, B, B), BF16),
            pltpu.VMEM((B, B), F32),
            pltpu.VMEM((4, B, 128), F32),
            pltpu.VMEM((128, n), F32),
            pltpu.VMEM((64, n), F32),
            dma((BLOCKS * SUB, 2)),
            dma((BLOCKS * SUB, 2)),
            dma((2, 2, 4)),
            dma((2, 2)),
            dma((8, 8 * SUB)),
            dma((3,)),
            dma((8,)),
            dma((5,)),
            dma((4,)),
            dma((2, 4)),
            dma((4,)),
            dma((4,)),
        ],
        compiler_params=pltpu.CompilerParams(
            collective_id=0, has_side_effects=True, vmem_limit_bytes=56 * 1024 * 1024
        ),
        name="solve_update",
    )(cross_cov, factor_cols, prior_cov)


def solution(mesh):
    placed = (P("row", "cand"), P("row", None), P("row", "cand"))
    return jax.shard_map(
        local,
        mesh=mesh,
        in_specs=placed,
        out_specs=(P("row", "cand"), P("row", "cand")),
        check_vma=False,
    )
```

time: 881 us -> 93.9 us (0.11)
  the two profiles are of different devices: /device:TPU:1 before, /device:TPU:4 now
where the time goes in v1:
time: 93.9 us; the launch traced here: 93.8 us
  Pallas kernels  87.6 us (93%)
  local copies, waits for them, and re-layouts  5.54 us (6%)
    pallas_call x1, Pallas kernels, local(): pl.pallas_call(kernel, out_shape=(jax.ShapeDtypeStruct((n, n), F32), jax....  87.6 us
    unnamed x4, local copies, waits for them, and re-layouts  5.54 us

profile of v1, /device:TPU:4, one launch (start us, length us, event | category | flops | bytes accessed | tf_op | source)
XLA Modules:
  0.0 93.8 jit_solution(709090650770943358)
XLA Ops:
  0.6 87.6 %solve_update.1 = (f32[1024,1024]{1,0:T(8,128)}, f32[64,1024]{1,0:T(8,128)}) custom-call(f32[1024,1024]{1,0:T(8,128)} %c_hbm.1, f32[1024,1024]{1,0:T(8,128)} %f_hbm.1, f32[64,1024]{1,0:T(8,128)} %p_hbm.1), custom_call_target="tpu_custom_call" | custom-call | tf_op jit(solution)/shard_map/solve_update/pallas_call | solution.py:451
  88.3 0.0 copy-start
  88.3 4.8 %copy.7 = f32[1024,1024]{1,0:T(8,128)} copy(f32[1024,1024]{1,0:T(8,128)} %get-tuple-element.4) | data formatting | bytes 8388608
  93.1 0.0 copy-done
  93.1 0.7 copy.8
Async XLA Ops:
  88.3 4.8 %copy-start = (f32[64,1024]{1,0:T(8,128)S(1)}, f32[64,1024]{1,0:T(8,128)}, u32[]{:S(2)}) copy-start(f32[64,1024]{1,0:T(8,128)} %get-tuple-element.5) | copy-start | bytes 786436

commit v2 on v0

v2 whole, which is shorter than its diff:
```python
import functools

import jax
import jax.numpy as jnp
from jax import lax
from jax.experimental import pallas as pl
from jax.experimental.pallas import tpu as pltpu
from jax.sharding import PartitionSpec as P

MESH = pl.DeviceIdType.MESH
F32, BF16 = jnp.float32, jnp.bfloat16
HIGHEST = lax.Precision.HIGHEST
B = 256
PIECE = 64
LAG = 2

TREES = (
    (2, 112, 98, 82, 74, 62, 46, 22, 48, 96, 112, 98, 86, 66, 48, 37, 65, 93, 96, 112, 98, 81, 96, 49, 80, 96, 112, 98, 82, 72, 49, 65),
    (1, 21, 45, 61, 69, 81, 97, 112, 48, 38, 48, 64, 81, 97, 112, 96, 66, 50, 96, 82, 97, 112, 96, 94, 80, 66, 50, 73, 89, 97, 112, 96),
    (8, 48, 64, 80, 96, 80, 64, 48, 48, 96, 82, 96, 112, 96, 81, 96, 40, 48, 73, 88, 104, 90, 74, 48, 27, 45, 61, 68, 84, 70, 62, 46),
    (4, 56, 64, 80, 96, 80, 64, 56, 23, 41, 61, 77, 88, 76, 62, 42, 36, 80, 70, 85, 100, 84, 69, 80, 48, 64, 80, 96, 112, 96, 80, 64),
)
STEP = ((0, 1), (0, 7), (1, 0), (3, 0))
FIRST = (1, 0, 3, 2)
NL = (0, 4)
NB = (8, 12)
BASE = (0, 8)
BLOCKS = 20
WAIT = LAG * 7
START = NL[1] + 1
UNITS = NB[1] + WAIT + 4


def b_index(q, s):
    return BASE[s // 2] + NL[s // 2] + 2 * q + s % 2


def split(x):
    hi = x.astype(BF16)
    return hi, (x - hi.astype(F32)).astype(BF16)


def dot(a, b):
    return jnp.dot(a, b, preferred_element_type=F32)


def dot3(ah, al, bh, bl):
    return dot(ah, bh) + (dot(ah, bl) + dot(al, bh))


def dotf(a, b):
    return jnp.dot(a, b, precision=HIGHEST, preferred_element_type=F32)


def invert_lower(d):
    ri = lax.broadcasted_iota(jnp.int32, (B, B), 0)
    ci = lax.broadcasted_iota(jnp.int32, (B, B), 1)
    same = ri == ci
    on_diag = jnp.where(same, d, 0.0)
    by_row = 1.0 / jnp.sum(on_diag, axis=1, keepdims=True)
    by_col = 1.0 / jnp.sum(on_diag, axis=0, keepdims=True)
    n = jnp.where(ri > ci, d, 0.0) * by_row
    inv = jnp.where(same, 1.0, 0.0) - jnp.where((ri >> 1) == (ci >> 1), n, 0.0)
    for k in range(1, 8):
        off = jnp.where(((ri >> (k + 1)) == (ci >> (k + 1))) & ((ri >> k) != (ci >> k)), n, 0.0)
        inv = inv - dotf(dotf(inv, off), inv)
    return inv * by_col


def kernel(
    c_hbm, f_hbm, p_hbm, out_hbm, post_hbm,
    w, fv, fh, fl, cv, pv, xh, xl, gh, gl, dsp, dv, lv, xb, sbt, tv,
    rs, sb, child_sem, sib_sem, own_sem, pre_s, pre_r, load_sem, raw_sem, out_sem, xr, xs, xsb, xss,
):
    row = lax.axis_index("row")
    x = lax.axis_index("cand")
    y = row >> 4
    z = (row >> 1) & 7
    core = row & 1

    def device(yy, zz, cc, xx=None):
        return ((yy & 3) * 16 + (zz & 7) * 2 + cc, x if xx is None else xx & 3)

    sibling = device(y, z, 1 - core)
    near = [[device(y + dy, z + dz, cc) for cc in range(2)] for dy, dz in STEP]
    near_same = [device(y + dy, z + dz, core) for dy, dz in STEP]
    beside = [device(y, z, core, x + dx) for dx in (1, 3)]

    def remote(src, dst, send_sem, recv_sem, to):
        return pltpu.make_async_remote_copy(
            src_ref=src, dst_ref=dst, send_sem=send_sem, recv_sem=recv_sem, device_id=to, device_id_type=MESH
        )

    load_f = pltpu.make_async_copy(f_hbm, fv, load_sem.at[0])
    load_c = pltpu.make_async_copy(c_hbm, cv, load_sem.at[1])
    load_p = pltpu.make_async_copy(p_hbm, pv, load_sem.at[2])

    def raw_copies(s):
        found = [(w.at[b_index(q, s)], c_hbm.at[pl.ds(0, B), pl.ds(q * B, B)]) for q in range(4)]
        for t in range(2 if s >= 2 else 0):
            found.append((w.at[BASE[1] + 2 * t + s % 2], f_hbm.at[pl.ds(0, B), pl.ds(t * B, B)]))
        if s % 2:
            found.append((lv, f_hbm.at[pl.ds(0, B), pl.ds((s - 1) * B, B)]))
        return [pltpu.make_async_copy(src, dst, raw_sem.at[i]) for i, (dst, src) in enumerate(found)]

    def load_d(s):
        return pltpu.make_async_copy(f_hbm.at[pl.ds(0, B), pl.ds(s * B, B)], dv, raw_sem.at[7])

    for s in range(4):

        @pl.when(row == s)
        def _(s=s):
            load_d(s).start()
            for c in raw_copies(s):
                c.start()

    barrier = pltpu.get_barrier_semaphore()
    for to in [t for pair in near for t in pair] + beside + [sibling]:
        pl.semaphore_signal(barrier, inc=1, device_id=to, device_id_type=MESH)
    load_f.start()
    load_c.start()
    load_p.start()

    for s in range(4):

        @pl.when(row == s)
        def _(s=s):
            load_d(s).wait()
            dsp[0], dsp[1] = split(invert_lower(dv[...]))
            for c in raw_copies(s):
                c.wait()
            if s % 2:
                dsp[2], dsp[3] = split(lv[...])

    def lookup(table, key):
        found = jnp.int32(0)
        for k, v in enumerate(table):
            found = jnp.where(key == k, v, found)
        return found

    is_root, depth, child = [], [], []
    for rho in range(2):
        idx = y * 8 + ((z - rho) & 7)
        merged = [TREES[2 * cc][k] + 128 * TREES[2 * cc + 1][k] for cc in range(2) for k in range(32)]
        v = lookup(merged, core * 32 + idx)
        is_root.append(idx == 0)
        depth.append(((v >> 4) & 7, v >> 11))
        child.append((v & 15, (v >> 7) & 15))

    p = (x - y) & 3
    qz = z >> 1
    lanes = pl.ds(pl.multiple_of((z & 1) * 128, 128), 128)
    relays = jnp.logical_or(jnp.logical_and(p == 1, core == 0), jnp.logical_and(p == 3, core == 1))
    onward = (beside[0][0], (x + jnp.where(core == 0, 1, 3)) & 3)
    x_lag = jnp.where(p == 2, 4, 2)

    pl.semaphore_wait(barrier, 11)

    def piece(b, tree):
        return w.at[b, pl.ds(pl.multiple_of(tree * 64, 64), PIECE)]

    def x_piece(s, tree):
        return xb.at[s, pl.ds(pl.multiple_of(tree * 64, 64), PIECE)]

    def needed(rho, n):
        m = n - NL[rho]
        return jnp.logical_and(m >= 0, (m >> 1) == qz), 2 * rho + (m & 1)

    def x_start(rho, il, n):
        hit, s = needed(rho, n)

        @pl.when(jnp.logical_and(p == 0, hit))
        def _():
            tree = 2 * core + il
            src = w.at[BASE[rho] + n, pl.ds(pl.multiple_of(tree * 64, 64), PIECE), lanes]
            for i in range(2):
                remote(src, x_piece(s, tree), xs.at[i, s, il], xr.at[s, il], beside[i]).start()

    def x_arrive(rho, il, n):
        hit, s = needed(rho, n)

        @pl.when(jnp.logical_and(p != 0, hit))
        def _():
            ref = x_piece(s, 2 * core + il)
            remote(ref, ref, xs.at[0, s, il], xr.at[s, il], sibling).wait_recv()

            @pl.when(relays)
            def _():
                remote(ref, ref, xs.at[0, s, il], xr.at[s, il], onward).start()

            remote(ref, ref, xss.at[s, il], xsb.at[s, il], sibling).start()

    def whole_copy(b, n):
        ref = w.at[b]
        return remote(ref, ref, pre_s.at[n >> 1], pre_r.at[n >> 1], sibling)

    def own_sends(b, slot):
        for tree in range(4):
            ref = w.at[b, pl.ds(64 * tree, PIECE)]
            yield remote(ref, ref, own_sem.at[slot, tree], rs.at[b, tree % 2], near[FIRST[tree]][tree // 2])

    def own_wait(slot):
        for copy in own_sends(0, slot):
            copy.wait_send()

    def own(rho, n):
        b = BASE[rho] + n
        j = n >> 1
        slot = j & 1

        @pl.when(core == 1)
        def _():
            whole_copy(b - 1, n).wait_recv()
            for il in range(2):
                x_start(rho, il, n - 1)
            w[b] = w[b] - dot3(dsp[2], dsp[3], *split(w[b - 1]))

        w[b] = dot3(dsp[0], dsp[1], *split(w[b]))
        whole_copy(b, n).start()

        @pl.when(j >= 2)
        def _():
            own_wait(slot)

        for copy in own_sends(b, slot):
            copy.start()
        for il in range(2):
            x_start(rho, il, n)

    def own_other(rho, n):
        whole_copy(BASE[rho] + n, n).wait_recv()
        for il in range(2):
            x_start(rho, il, n)

    def forward(rho, il, n):
        b = BASE[rho] + n
        ref = piece(b, 2 * core + il)
        remote(ref, ref, sib_sem.at[rho, il], rs.at[b, il], sibling).wait_recv()
        for d in range(4):

            @pl.when(((child[rho][il] >> d) & 1) == 1)
            def _(d=d):
                remote(ref, ref, child_sem.at[rho, il, d], rs.at[b, il], near_same[d]).start()

    def share(rho, il, n):
        b = BASE[rho] + n
        ref = piece(b, 2 * core + il)
        remote(ref, ref, sib_sem.at[rho, il], sb.at[b, il], sibling).start()
        x_start(rho, il, n)

    def wait_other(rho, n):
        b = BASE[rho] + n

        @pl.when(jnp.logical_not(is_root[rho]))
        def _():
            for il in range(2):
                ref = piece(b, 2 * (1 - core) + il)
                remote(ref, ref, sib_sem.at[rho, il], sb.at[b, il], sibling).wait_recv()

    def take_g(n):
        wait_other(1, n)
        half, t = n % 2, n // 2
        rows, cols = pl.ds(half * B, B), pl.ds(t * B, B)
        gh[rows, cols], gl[rows, cols] = split(w[BASE[1] + n])

    def finish(y2, y3, hi, lo):
        r = dot3(gh[...], gl[...], hi, lo)
        return y2 - r[:B], y3 - r[B:]

    def columns(q):
        return pl.ds(pl.multiple_of(q * B, B), B)

    def solve_group(q):
        cols = columns(q)
        for s in range(4):
            wait_other(s // 2, b_index(q, s) - BASE[s // 2])
        first = [w[b_index(q, s)] for s in range(2)]
        for s in range(2):
            xh[pl.ds(s * B, B), cols], xl[pl.ds(s * B, B), cols] = split(first[s])
        top = pl.ds(0, 2 * B)
        last = finish(w[b_index(q, 2)], w[b_index(q, 3)], xh[top, cols], xl[top, cols])
        for s in range(2, 4):
            xh[pl.ds(s * B, B), cols], xl[pl.ds(s * B, B), cols] = split(last[s - 2])
        for s, v in enumerate([*first, *last]):

            @pl.when(row == s)
            def _(v=v):
                dv[...] = v

    def update_group(q, part):
        cols = columns(q)
        for m in range(2 * part, 2 * part + 2):
            rows = pl.ds(m * B, B)
            cv[rows, cols] = cv[rows, cols] - dot3(fh[rows, :], fl[rows, :], xh[:, cols], xl[:, cols])

        if part == 0:

            @pl.when(row < 4)
            def _():
                cv[pl.ds(0, B), cols] = dv[...]

        else:
            pltpu.make_async_copy(cv.at[:, cols], out_hbm.at[:, cols], out_sem.at[q]).start()

    def step(u, carry):
        for rho in range(2):

            @pl.when(jnp.logical_and(is_root[rho], jnp.logical_and(u < NB[rho], (u & 1) == core)))
            def _(rho=rho):
                own(rho, u)

            late = u - 2
            odd = jnp.logical_and(core == 0, (late & 1) == 1)

            @pl.when(jnp.logical_and(jnp.logical_and(is_root[rho], odd), jnp.logical_and(late >= 0, late < NB[rho])))
            def _(rho=rho, late=late):
                own_other(rho, late)

        for act in (forward, share):
            for rho in range(2):
                for il in range(2):
                    n = u - LAG * depth[rho][il]
                    theirs = jnp.logical_not(is_root[rho])

                    @pl.when(jnp.logical_and(jnp.logical_and(n >= 0, n < NB[rho]), theirs))
                    def _(act=act, rho=rho, il=il, n=n):
                        act(rho, il, n)

        for rho in range(2):
            for il in range(2):
                n = u - LAG * depth[rho][il] - x_lag

                @pl.when(jnp.logical_and(n >= 0, n < NB[rho]))
                def _(rho=rho, il=il, n=n):
                    x_arrive(rho, il, n)

        @pl.when(u == 0)
        def _():
            load_f.wait()

        @pl.when(u < 16)
        def _():
            rows = pl.ds(pl.multiple_of(u * 64, 64), 64)
            hi, lo = split(fv[rows, :])
            fh[rows, :] = hi
            fl[rows, :] = lo

        for n in range(NL[1]):

            @pl.when(u == WAIT + n)
            def _(n=n):
                take_g(n)

        @pl.when(u == WAIT)
        def _():
            load_c.wait()

        g = u - WAIT - START

        @pl.when(jnp.logical_and(g >= 0, g < 8))
        def _():
            q = g >> 1

            @pl.when((g & 1) == 0)
            def _():
                solve_group(q)
                update_group(q, 0)

            @pl.when((g & 1) == 1)
            def _():
                update_group(q, 1)

        return carry

    lax.fori_loop(0, UNITS, step, 0)

    @pl.when(p == 0)
    def _():
        for s in range(4):
            xb[s] = w[b_index(qz, s), :, lanes]

    @pl.when(p != 0)
    def _():
        for s in range(4):
            for il in range(2):
                ref = x_piece(s, 2 * (1 - core) + il)
                remote(ref, ref, xss.at[s, il], xsb.at[s, il], sibling).wait_recv()

    parts = [split(xb[s]) for s in range(2)]
    hi, lo = (jnp.concatenate([parts[0][i], parts[1][i]], axis=0) for i in range(2))
    for s, v in enumerate([xb[0], xb[1], *finish(xb[2], xb[3], hi, lo)]):
        sbt[:, pl.ds(s * B, B)] = v.T
    load_p.wait()
    sh, sl = split(sbt[pl.ds(pl.multiple_of(core * 64, 64), 64), :])

    for q in range(4):
        cols = pl.ds(q * B, B)
        tv[:, cols] = pv[:, cols] - dot3(sh, sl, xh[:, cols], xl[:, cols])

    save_p = pltpu.make_async_copy(tv, post_hbm, out_sem.at[4])
    save_p.start()

    for rho in range(2):
        whole = w.at[pl.ds(0, NB[rho]), pl.ds(0, PIECE)]

        @pl.when(is_root[rho])
        def _(rho=rho):
            own_wait(0)
            own_wait(1)
            for j in range(NB[rho] // 2):
                whole_copy(0, 2 * j).wait_send()

        @pl.when(jnp.logical_not(is_root[rho]))
        def _(rho=rho, whole=whole):
            for il in range(2):
                for d in range(4):

                    @pl.when(((child[rho][il] >> d) & 1) == 1)
                    def _(il=il, d=d):
                        remote(whole, whole, child_sem.at[rho, il, d], rs.at[0, il], near_same[d]).wait_send()

                remote(whole, whole, sib_sem.at[rho, il], rs.at[0, il], sibling).wait_send()

    def x_sent(i, s, il):
        ref = x_piece(s, 2 * core + il)
        remote(ref, ref, xs.at[i, s, il], xr.at[s, il], sibling).wait_send()

    for s in range(4):
        for il in range(2):

            @pl.when(p == 0)
            def _(s=s, il=il):
                x_sent(0, s, il)
                x_sent(1, s, il)

            @pl.when(relays)
            def _(s=s, il=il):
                x_sent(0, s, il)

            @pl.when(p != 0)
            def _(s=s, il=il):
                ref = x_piece(s, 2 * core + il)
                remote(ref, ref, xss.at[s, il], xsb.at[s, il], sibling).wait_send()

    save_p.wait()
    for q in range(4):
        cols = pl.ds(q * B, B)
        pltpu.make_async_copy(cv.at[:, cols], out_hbm.at[:, cols], out_sem.at[q]).wait()


def local(cross_cov, factor_cols, prior_cov):
    n = 1024
    dma = pltpu.SemaphoreType.DMA
    any_space = pl.BlockSpec(memory_space=pl.ANY)
    return pl.pallas_call(
        kernel,
        out_shape=(jax.ShapeDtypeStruct((n, n), F32), jax.ShapeDtypeStruct((64, n), F32)),
        in_specs=[any_space] * 3,
        out_specs=(any_space, any_space),
        scratch_shapes=[
            pltpu.VMEM((BLOCKS, B, B), F32),
            pltpu.VMEM((n, n), F32),
            pltpu.VMEM((n, n), BF16),
            pltpu.VMEM((n, n), BF16),
            pltpu.VMEM((n, n), F32),
            pltpu.VMEM((64, n), F32),
            pltpu.VMEM((n, n), BF16),
            pltpu.VMEM((n, n), BF16),
            pltpu.VMEM((2 * B, 2 * B), BF16),
            pltpu.VMEM((2 * B, 2 * B), BF16),
            pltpu.VMEM((4, B, B), BF16),
            pltpu.VMEM((B, B), F32),
            pltpu.VMEM((B, B), F32),
            pltpu.VMEM((4, B, 128), F32),
            pltpu.VMEM((128, n), F32),
            pltpu.VMEM((64, n), F32),
            dma((BLOCKS, 2)),
            dma((BLOCKS, 2)),
            dma((2, 2, 4)),
            dma((2, 2)),
            dma((2, 4)),
            dma((6,)),
            dma((6,)),
            dma((3,)),
            dma((8,)),
            dma((5,)),
            dma((4, 2)),
            dma((2, 4, 2)),
            dma((4, 2)),
            dma((4, 2)),
        ],
        compiler_params=pltpu.CompilerParams(
            collective_id=0, has_side_effects=True, vmem_limit_bytes=56 * 1024 * 1024
        ),
        name="solve_update",
    )(cross_cov, factor_cols, prior_cov)


def solution(mesh):
    placed = (P("row", "cand"), P("row", None), P("row", "cand"))
    return jax.shard_map(
        local,
        mesh=mesh,
        in_specs=placed,
        out_specs=(P("row", "cand"), P("row", "cand")),
        check_vma=False,
    )
```

time: 881 us -> 72.8 us (0.08)
  waiting for transfers between devices: 700 us -> 0 us
  other arithmetic: 97.6 us -> 0 us
  Pallas kernels: 0 us -> 66.5 us
  matrix products: 50.5 us -> 0 us
  between operations: 14.1 us -> 0.65 us
  local copies, waits for them, and re-layouts: 15.6 us -> 5.54 us
    psum x5 -> x0, waiting for transfers between devices: 700 us -> none  [broadcast(): return lax.psum(jnp.where(mine, x, jnp.zeros_like(x)), axis)]
    another operation x6 -> x0, other arithmetic: 80 us -> none  [solve_lower(): lax.linalg.triangular_solve(diagonal, values, left_side=True, lower=True)]
    pallas_call x0 -> x1, Pallas kernels: none -> 66.5 us  [local(): pl.pallas_call(kernel, out_shape=(jax.ShapeDtypeStruct((n, n), F32), jax....]
    dot_general x8 -> x0, matrix products: 41.1 us -> none  [the longest x4 34.5 us: local(): jnp.dot(factor_block, solution, precision=highest_precision, preferred_el...]
    another operation x29 -> x0, local copies, waits for them, and re-layouts: 15.6 us -> none  [solve_lower(): lax.linalg.triangular_solve(diagonal, values, left_side=True, lower=True)]
    scatter x4 -> x0, other arithmetic: 9.44 us -> none  [local(): current.at[:PANEL]]
    another operation x12 -> x0, matrix products: 9.44 us -> none  [solve_lower(): lax.linalg.triangular_solve(diagonal, values, left_side=True, lower=True)]
  transfers between devices with their start and end apart: 5 -> 0, of which waited for: 5 -> 0; matrix products, arithmetic and copies ran while one was open for 10% -> 0% of each run, Pallas kernels for 0% -> 0%
where the time goes in v2:
time: 72.8 us; the launch traced here: 72.7 us
  Pallas kernels  66.5 us (91%)
  local copies, waits for them, and re-layouts  5.54 us (8%)
    pallas_call x1, Pallas kernels, local(): pl.pallas_call(kernel, out_shape=(jax.ShapeDtypeStruct((n, n), F32), jax....  66.5 us
    unnamed x4, local copies, waits for them, and re-layouts  5.54 us

profile of v2, /device:TPU:1, one launch (start us, length us, event | category | flops | bytes accessed | tf_op | source)
XLA Modules:
  0.0 72.7 jit_solution(4225920686831591250)
XLA Ops:
  0.6 66.5 %solve_update.1 = (f32[1024,1024]{1,0:T(8,128)}, f32[64,1024]{1,0:T(8,128)}) custom-call(f32[1024,1024]{1,0:T(8,128)} %c_hbm.1, f32[1024,1024]{1,0:T(8,128)} %f_hbm.1, f32[64,1024]{1,0:T(8,128)} %p_hbm.1), custom_call_target="tpu_custom_call" | custom-call | tf_op jit(solution)/shard_map/solve_update/pallas_call | solution.py:455
  67.2 0.0 copy-start
  67.2 4.8 %copy.7 = f32[1024,1024]{1,0:T(8,128)} copy(f32[1024,1024]{1,0:T(8,128)} %get-tuple-element.4) | data formatting | bytes 8388608
  72.0 0.0 copy-done
  72.0 0.7 copy.8
Async XLA Ops:
  67.2 4.8 %copy-start = (f32[64,1024]{1,0:T(8,128)S(1)}, f32[64,1024]{1,0:T(8,128)}, u32[]{:S(2)}) copy-start(f32[64,1024]{1,0:T(8,128)} %get-tuple-element.5) | copy-start | bytes 786436

commit v3 on v2

--- a/solution.py
+++ b/solution.py
@@ -27,8 +27,8 @@
 BASE = (0, 8)
 BLOCKS = 20
 WAIT = LAG * 7
-START = NL[1] + 1
-UNITS = NB[1] + WAIT + 4
+STEPS = (8, 10)
+UNITS = STEPS[1] + WAIT + 4
 
 
 def b_index(q, s):
@@ -52,25 +52,36 @@
     return jnp.dot(a, b, precision=HIGHEST, preferred_element_type=F32)
 
 
-def invert_lower(d):
-    ri = lax.broadcasted_iota(jnp.int32, (B, B), 0)
-    ci = lax.broadcasted_iota(jnp.int32, (B, B), 1)
+def invert_block(d):
+    n = d.shape[0]
+    ri = lax.broadcasted_iota(jnp.int32, (n, n), 0)
+    ci = lax.broadcasted_iota(jnp.int32, (n, n), 1)
     same = ri == ci
     on_diag = jnp.where(same, d, 0.0)
     by_row = 1.0 / jnp.sum(on_diag, axis=1, keepdims=True)
     by_col = 1.0 / jnp.sum(on_diag, axis=0, keepdims=True)
-    n = jnp.where(ri > ci, d, 0.0) * by_row
-    inv = jnp.where(same, 1.0, 0.0) - jnp.where((ri >> 1) == (ci >> 1), n, 0.0)
-    for k in range(1, 8):
-        off = jnp.where(((ri >> (k + 1)) == (ci >> (k + 1))) & ((ri >> k) != (ci >> k)), n, 0.0)
+    low = jnp.where(ri > ci, d, 0.0) * by_row
+    inv = jnp.where(same, 1.0, 0.0) - jnp.where((ri >> 1) == (ci >> 1), low, 0.0)
+    k = 1
+    while 2 << k <= n:
+        off = jnp.where(((ri >> (k + 1)) == (ci >> (k + 1))) & ((ri >> k) != (ci >> k)), low, 0.0)
         inv = inv - dotf(dotf(inv, off), inv)
+        k += 1
     return inv * by_col
 
 
+def invert_lower(d):
+    h = B // 2
+    first, last = invert_block(d[:h, :h]), invert_block(d[h:, h:])
+    corner = -dotf(dotf(last, d[h:, :h]), first)
+    top = jnp.concatenate([first, jnp.zeros((h, h), F32)], axis=1)
+    return jnp.concatenate([top, jnp.concatenate([corner, last], axis=1)], axis=0)
+
+
 def kernel(
-    c_hbm, f_hbm, p_hbm, out_hbm, post_hbm,
-    w, fv, fh, fl, cv, pv, xh, xl, gh, gl, dsp, dv, lv, xb, sbt, tv,
-    rs, sb, child_sem, sib_sem, own_sem, pre_s, pre_r, load_sem, raw_sem, out_sem, xr, xs, xsb, xss,
+    c_hbm, f_hbm, p_hbm, cv, tv,
+    w, fv, fh, fl, pv, xh, xl, gh, gl, dsp, dv, lv, xb, sbt,
+    rs, sb, child_sem, sib_sem, own_sem, pre_s, pre_r, load_sem, raw_sem, xr, xs, xsb, xss,
 ):
     row = lax.axis_index("row")
     x = lax.axis_index("cand")
@@ -270,67 +281,73 @@
     def columns(q):
         return pl.ds(pl.multiple_of(q * B, B), B)
 
-    def solve_group(q):
+    def update(q, half):
         cols = columns(q)
-        for s in range(4):
-            wait_other(s // 2, b_index(q, s) - BASE[s // 2])
-        first = [w[b_index(q, s)] for s in range(2)]
+        depth_part = pl.ds(half * 2 * B, 2 * B)
+        for m in range(4):
+            rows = pl.ds(m * B, B)
+            cv[rows, cols] = cv[rows, cols] - dot3(
+                fh[rows, depth_part], fl[rows, depth_part], xh[depth_part, cols], xl[depth_part, cols]
+            )
+
+    def first_half(q):
+        cols = columns(q)
         for s in range(2):
-            xh[pl.ds(s * B, B), cols], xl[pl.ds(s * B, B), cols] = split(first[s])
+            wait_other(0, 2 * q + s)
+            xh[pl.ds(s * B, B), cols], xl[pl.ds(s * B, B), cols] = split(w[b_index(q, s)])
+        update(q, 0)
+
+    def second_half(q):
+        cols = columns(q)
+        for s in range(2, 4):
+            wait_other(1, b_index(q, s) - BASE[1])
         top = pl.ds(0, 2 * B)
         last = finish(w[b_index(q, 2)], w[b_index(q, 3)], xh[top, cols], xl[top, cols])
         for s in range(2, 4):
             xh[pl.ds(s * B, B), cols], xl[pl.ds(s * B, B), cols] = split(last[s - 2])
-        for s, v in enumerate([*first, *last]):
+        update(q, 1)
+        for s in range(4):
 
             @pl.when(row == s)
-            def _(v=v):
-                dv[...] = v
-
-    def update_group(q, part):
-        cols = columns(q)
-        for m in range(2 * part, 2 * part + 2):
-            rows = pl.ds(m * B, B)
-            cv[rows, cols] = cv[rows, cols] - dot3(fh[rows, :], fl[rows, :], xh[:, cols], xl[:, cols])
-
-        if part == 0:
-
-            @pl.when(row < 4)
-            def _():
-                cv[pl.ds(0, B), cols] = dv[...]
-
-        else:
-            pltpu.make_async_copy(cv.at[:, cols], out_hbm.at[:, cols], out_sem.at[q]).start()
+            def _(s=s):
+                cv[pl.ds(0, B), cols] = w[b_index(q, s)] if s < 2 else last[s - 2]
 
     def step(u, carry):
+        def blocks_at(rho, v):
+            inside = jnp.logical_and(v >= 0, v < STEPS[rho])
+            if rho == 0:
+                return [(inside, v)]
+            early = jnp.logical_and(v >= 0, v < 2)
+            return [(inside, jnp.where(early, 2 * v, v + 2)), (early, 2 * v + 1)]
+
         for rho in range(2):
-
-            @pl.when(jnp.logical_and(is_root[rho], jnp.logical_and(u < NB[rho], (u & 1) == core)))
-            def _(rho=rho):
-                own(rho, u)
-
-            late = u - 2
-            odd = jnp.logical_and(core == 0, (late & 1) == 1)
-
-            @pl.when(jnp.logical_and(jnp.logical_and(is_root[rho], odd), jnp.logical_and(late >= 0, late < NB[rho])))
-            def _(rho=rho, late=late):
-                own_other(rho, late)
+            for inside, n in blocks_at(rho, u):
+
+                @pl.when(jnp.logical_and(is_root[rho], jnp.logical_and(inside, (n & 1) == core)))
+                def _(rho=rho, n=n):
+                    own(rho, n)
+
+            for inside, n in blocks_at(rho, u - 2):
+                odd = jnp.logical_and(core == 0, (n & 1) == 1)
+
+                @pl.when(jnp.logical_and(is_root[rho], jnp.logical_and(inside, odd)))
+                def _(rho=rho, n=n):
+                    own_other(rho, n)
 
         for act in (forward, share):
             for rho in range(2):
                 for il in range(2):
-                    n = u - LAG * depth[rho][il]
-                    theirs = jnp.logical_not(is_root[rho])
-
-                    @pl.when(jnp.logical_and(jnp.logical_and(n >= 0, n < NB[rho]), theirs))
-                    def _(act=act, rho=rho, il=il, n=n):
-                        act(rho, il, n)
+                    for inside, n in blocks_at(rho, u - LAG * depth[rho][il]):
+
+                        @pl.when(jnp.logical_and(inside, jnp.logical_not(is_root[rho])))
+                        def _(act=act, rho=rho, il=il, n=n):
+                            act(rho, il, n)
 
         for rho in range(2):
             for il in range(2):
-                n = u - LAG * depth[rho][il] - x_lag
-
-                @pl.when(jnp.logical_and(n >= 0, n < NB[rho]))
+                inside, n = blocks_at(rho, u - LAG * depth[rho][il] - x_lag)[0]
+
+                @pl.when(inside)
                 def _(rho=rho, il=il, n=n):
                     x_arrive(rho, il, n)
 
@@ -347,7 +364,7 @@
 
         for n in range(NL[1]):
 
-            @pl.when(u == WAIT + n)
+            @pl.when(u == WAIT + n // 2)
             def _(n=n):
                 take_g(n)
 
@@ -355,20 +372,17 @@
         def _():
             load_c.wait()
 
-        g = u - WAIT - START
-
-        @pl.when(jnp.logical_and(g >= 0, g < 8))
-        def _():
-            q = g >> 1
-
-            @pl.when((g & 1) == 0)
-            def _():
-                solve_group(q)
-                update_group(q, 0)
-
-            @pl.when((g & 1) == 1)
-            def _():
-                update_group(q, 1)
+        g = u - WAIT
+
+        @pl.when(jnp.logical_and((g & 1) == 1, jnp.logical_and(g >= 1, g < 8)))
+        def _():
+            first_half(g >> 1)
+
+        second = jnp.logical_and((g & 1) == 0, jnp.logical_and(g >= 4, g < 9))
+
+        @pl.when(jnp.logical_or(second, g == 9))
+        def _():
+            second_half((g - 3) >> 1)
 
         return carry
 
@@ -397,9 +411,6 @@
         cols = pl.ds(q * B, B)
         tv[:, cols] = pv[:, cols] - dot3(sh, sl, xh[:, cols], xl[:, cols])
 
-    save_p = pltpu.make_async_copy(tv, post_hbm, out_sem.at[4])
-    save_p.start()
-
     for rho in range(2):
         whole = w.at[pl.ds(0, NB[rho]), pl.ds(0, PIECE)]
 
@@ -442,27 +453,21 @@
                 ref = x_piece(s, 2 * core + il)
                 remote(ref, ref, xss.at[s, il], xsb.at[s, il], sibling).wait_send()
 
-    save_p.wait()
-    for q in range(4):
-        cols = pl.ds(q * B, B)
-        pltpu.make_async_copy(cv.at[:, cols], out_hbm.at[:, cols], out_sem.at[q]).wait()
-
 
 def local(cross_cov, factor_cols, prior_cov):
     n = 1024
     dma = pltpu.SemaphoreType.DMA
-    any_space = pl.BlockSpec(memory_space=pl.ANY)
-    return pl.pallas_call(
+    in_hbm = pl.BlockSpec(memory_space=pltpu.HBM)
+    current, posterior = pl.pallas_call(
         kernel,
-        out_shape=(jax.ShapeDtypeStruct((n, n), F32), jax.ShapeDtypeStruct((64, n), F32)),
-        in_specs=[any_space] * 3,
-        out_specs=(any_space, any_space),
+        out_shape=(pltpu.VMEM((n, n), F32), pltpu.VMEM((64, n), F32)),
+        in_specs=[in_hbm] * 3,
+        out_specs=(pl.BlockSpec(memory_space=pltpu.VMEM),) * 2,
         scratch_shapes=[
             pltpu.VMEM((BLOCKS, B, B), F32),
             pltpu.VMEM((n, n), F32),
             pltpu.VMEM((n, n), BF16),
             pltpu.VMEM((n, n), BF16),
-            pltpu.VMEM((n, n), F32),
             pltpu.VMEM((64, n), F32),
             pltpu.VMEM((n, n), BF16),
             pltpu.VMEM((n, n), BF16),
@@ -473,7 +478,6 @@
             pltpu.VMEM((B, B), F32),
             pltpu.VMEM((4, B, 128), F32),
             pltpu.VMEM((128, n), F32),
-            pltpu.VMEM((64, n), F32),
             dma((BLOCKS, 2)),
             dma((BLOCKS, 2)),
             dma((2, 2, 4)),
@@ -483,17 +487,41 @@
             dma((6,)),
             dma((3,)),
             dma((8,)),
-            dma((5,)),
             dma((4, 2)),
             dma((2, 4, 2)),
             dma((4, 2)),
             dma((4, 2)),
         ],
         compiler_params=pltpu.CompilerParams(
-            collective_id=0, has_side_effects=True, vmem_limit_bytes=56 * 1024 * 1024
+            collective_id=0, has_side_effects=True, vmem_limit_bytes=int(59.5 * 1024 * 1024)
         ),
         name="solve_update",
     )(cross_cov, factor_cols, prior_cov)
+    return hand_on(current, posterior)
+
+
+def hand_on_kernel(a_in, b_in, a_out, b_out, sem):
+    rows = 256
+    copies = [
+        pltpu.make_async_copy(a_in.at[pl.ds(i * rows, rows)], a_out.at[pl.ds(i * rows, rows)], sem.at[i])
+        for i in range(4)
+    ]
+    copies.append(pltpu.make_async_copy(b_in, b_out, sem.at[4]))
+    for c in copies:
+        c.start()
+    for c in copies:
+        c.wait()
+
+
+def hand_on(current, posterior):
+    return pl.pallas_call(
+        hand_on_kernel,
+        out_shape=(jax.ShapeDtypeStruct(current.shape, F32), jax.ShapeDtypeStruct(posterior.shape, F32)),
+        in_specs=[pl.BlockSpec(memory_space=pltpu.VMEM)] * 2,
+        out_specs=(pl.BlockSpec(memory_space=pltpu.HBM),) * 2,
+        scratch_shapes=[pltpu.SemaphoreType.DMA((5,))],
+        name="hand_on",
+    )(current, posterior)
 
 
 def solution(mesh):

time: 72.8 us -> 70.7 us (0.971)
  local copies, waits for them, and re-layouts: 5.54 us -> 2.62 us
    unnamed x4, local copies, waits for them, and re-layouts: 5.54 us -> 2.62 us
    pallas_call x1 -> x2, Pallas kernels: 66.5 us -> 67.2 us  [the longest x1 62.9 us: local(): pl.pallas_call(kernel, out_shape=(pltpu.VMEM((n, n), F32), pltpu.VMEM((64...]
where the time goes in v3:
time: 70.7 us
  Pallas kernels  67.2 us (95%)
  local copies, waits for them, and re-layouts  2.62 us (4%)
  between operations  0.81 us (1%)
    pallas_call x1, Pallas kernels, local(): pl.pallas_call(kernel, out_shape=(pltpu.VMEM((n, n), F32), pltpu.VMEM((64...  62.9 us
    pallas_call x1, Pallas kernels, hand_on(): pl.pallas_call(hand_on_kernel, out_shape=(jax.ShapeDtypeStruct(current.sh...  4.34 us
    unnamed x4, local copies, waits for them, and re-layouts  2.62 us

profile of v3, /device:TPU:1, one launch (start us, length us, event | category | flops | bytes accessed | tf_op | source)
XLA Modules:
  0.0 70.7 jit_solution(2156668036479569245)
XLA Ops:
  0.6 62.9 %solve_update.1 = (f32[1024,1024]{1,0:T(8,128)S(1)}, f32[64,1024]{1,0:T(8,128)S(1)}) custom-call(f32[1024,1024]{1,0:T(8,128)} %c_hbm.1, f32[1024,1024]{1,0:T(8,128)} %f_hbm.1, f32[64,1024]{1,0:T(8,128)} %p_hbm.1), custom_call_target="tpu_custom_call" | custom-call | tf_op jit(solution)/shard_map/solve_update/pallas_call | solution.py:461
  63.5 0.0 copy-start
  63.5 1.9 %copy-done = f32[1024,1024]{1,0:T(8,128)} copy-done((f32[1024,1024]{1,0:T(8,128)}, f32[1024,1024]{1,0:T(8,128)S(1)}, u32[]{:S(2)}) %copy-start) | copy-done | bytes 4194328
  65.5 0.0 copy-start.1
  65.5 0.7 copy-done.1
  66.2 4.3 %hand_on.1 = (f32[1024,1024]{1,0:T(8,128)}, f32[64,1024]{1,0:T(8,128)}) custom-call(f32[1024,1024]{1,0:T(8,128)} %copy-done, f32[64,1024]{1,0:T(8,128)} %copy-done.1), custom_call_target="tpu_custom_call" | custom-call | tf_op jit(solution)/shard_map/hand_on/pallas_call | solution.py:517
Async XLA Ops:
  63.5 1.9 %copy-start = (f32[1024,1024]{1,0:T(8,128)}, f32[1024,1024]{1,0:T(8,128)S(1)}, u32[]{:S(2)}) copy-start(f32[1024,1024]{1,0:T(8,128)S(1)} %get-tuple-element.4.a_in) | copy-start | bytes 12582916
  65.5 0.7 copy-start.1

commit v4 on v3

--- a/solution.py
+++ b/solution.py
@@ -520,6 +520,7 @@
         in_specs=[pl.BlockSpec(memory_space=pltpu.VMEM)] * 2,
         out_specs=(pl.BlockSpec(memory_space=pltpu.HBM),) * 2,
         scratch_shapes=[pltpu.SemaphoreType.DMA((5,))],
+        compiler_params=pltpu.CompilerParams(vmem_limit_bytes=8 * 1024 * 1024),
         name="hand_on",
     )(current, posterior)
 

time: 70.7 us -> 65.9 us (0.932)
  local copies, waits for them, and re-layouts: 2.62 us -> 0 us
  Pallas kernels: 67.2 us -> 65 us
    unnamed x4 -> x0, local copies, waits for them, and re-layouts: 2.62 us -> none
    pallas_call x1, Pallas kernels: 4.34 us -> 2.13 us  [hand_on(): pl.pallas_call(hand_on_kernel, out_shape=(jax.ShapeDtypeStruct(current.sh...]
where the time goes in v4:
time: 65.9 us; the launch traced here: 65.8 us
  Pallas kernels  65 us (99%)
  between operations  0.8 us (1%)
    pallas_call x1, Pallas kernels, local(): pl.pallas_call(kernel, out_shape=(pltpu.VMEM((n, n), F32), pltpu.VMEM((64...  62.9 us
    pallas_call x1, Pallas kernels, hand_on(): pl.pallas_call(hand_on_kernel, out_shape=(jax.ShapeDtypeStruct(current.sh...  2.13 us

profile of v4, /device:TPU:1, one launch (start us, length us, event | category | flops | bytes accessed | tf_op | source)
XLA Modules:
  0.0 65.8 jit_solution(12457912412890395534)
XLA Ops:
  0.6 62.9 %solve_update.1 = (f32[1024,1024]{1,0:T(8,128)S(1)}, f32[64,1024]{1,0:T(8,128)S(1)}) custom-call(f32[1024,1024]{1,0:T(8,128)} %c_hbm.1, f32[1024,1024]{1,0:T(8,128)} %f_hbm.1, f32[64,1024]{1,0:T(8,128)} %p_hbm.1), custom_call_target="tpu_custom_call" | custom-call | tf_op jit(solution)/shard_map/solve_update/pallas_call | solution.py:461
  63.5 2.1 %hand_on.1 = (f32[1024,1024]{1,0:T(8,128)}, f32[64,1024]{1,0:T(8,128)}) custom-call(f32[1024,1024]{1,0:T(8,128)S(1)} %get-tuple-element.4.a_in, f32[64,1024]{1,0:T(8,128)S(1)} %get-tuple-element.5.b_in), custom_call_target="tpu_custom_call" | custom-call | tf_op jit(solution)/shard_map/hand_on/pallas_call | solution.py:517

commit v5 on v4

--- a/solution.py
+++ b/solution.py
@@ -65,7 +65,8 @@
     k = 1
     while 2 << k <= n:
         off = jnp.where(((ri >> (k + 1)) == (ci >> (k + 1))) & ((ri >> k) != (ci >> k)), low, 0.0)
-        inv = inv - dotf(dotf(inv, off), inv)
+        parts = split(inv)
+        inv = inv - dot3(*split(dot3(*parts, *split(off))), *parts)
         k += 1
     return inv * by_col
 
@@ -80,7 +81,7 @@
 
 def kernel(
     c_hbm, f_hbm, p_hbm, cv, tv,
-    w, fv, fh, fl, pv, xh, xl, gh, gl, dsp, dv, lv, xb, sbt,
+    w, fv, fh, fl, pv, xh, xl, gh, gl, dsp, dv, lv, xb, rb, sbt,
     rs, sb, child_sem, sib_sem, own_sem, pre_s, pre_r, load_sem, raw_sem, xr, xs, xsb, xss,
 ):
     row = lax.axis_index("row")
@@ -312,6 +313,43 @@
             def _(s=s):
                 cv[pl.ds(0, B), cols] = w[b_index(q, s)] if s < 2 else last[s - 2]
 
+    def x_take(s):
+        @pl.when(p == 0)
+        def _():
+            xb[s] = w[b_index(qz, s), :, lanes]
+
+        @pl.when(p != 0)
+        def _():
+            for il in range(2):
+                ref = x_piece(s, 2 * (1 - core) + il)
+                remote(ref, ref, xss.at[s, il], xsb.at[s, il], sibling).wait_recv()
+
+    mine = pl.ds(pl.multiple_of(core * 64, 64), 64)
+
+    def downdate(before, half):
+        part = pl.ds(half * 2 * B, 2 * B)
+        sh, sl = split(sbt[mine, part])
+        for q in range(4):
+            cols = pl.ds(q * B, B)
+            tv[:, cols] = before[:, cols] - dot3(sh, sl, xh[part, cols], xl[part, cols])
+
+    def posterior_first():
+        parts = []
+        for s in range(2):
+            x_take(s)
+            parts.append(split(xb[s]))
+            sbt[:, pl.ds(s * B, B)] = xb[s].T
+        hi, lo = (jnp.concatenate([parts[0][i], parts[1][i]], axis=0) for i in range(2))
+        rb[...] = dot3(gh[...], gl[...], hi, lo)
+        load_p.wait()
+        downdate(pv, 0)
+
+    def posterior_second():
+        for s in range(2, 4):
+            x_take(s)
+            sbt[:, pl.ds(s * B, B)] = (xb[s] - rb[pl.ds((s - 2) * B, B), :]).T
+        downdate(tv, 1)
+
     def step(u, carry):
         def blocks_at(rho, v):
             inside = jnp.logical_and(v >= 0, v < STEPS[rho])
@@ -384,32 +422,15 @@
         def _():
             second_half((g - 3) >> 1)
 
+        @pl.when(g == 12)
+        def _():
+            posterior_first()
+
         return carry
 
     lax.fori_loop(0, UNITS, step, 0)
 
-    @pl.when(p == 0)
-    def _():
-        for s in range(4):
-            xb[s] = w[b_index(qz, s), :, lanes]
-
-    @pl.when(p != 0)
-    def _():
-        for s in range(4):
-            for il in range(2):
-                ref = x_piece(s, 2 * (1 - core) + il)
-                remote(ref, ref, xss.at[s, il], xsb.at[s, il], sibling).wait_recv()
-
-    parts = [split(xb[s]) for s in range(2)]
-    hi, lo = (jnp.concatenate([parts[0][i], parts[1][i]], axis=0) for i in range(2))
-    for s, v in enumerate([xb[0], xb[1], *finish(xb[2], xb[3], hi, lo)]):
-        sbt[:, pl.ds(s * B, B)] = v.T
-    load_p.wait()
-    sh, sl = split(sbt[pl.ds(pl.multiple_of(core * 64, 64), 64), :])
-
-    for q in range(4):
-        cols = pl.ds(q * B, B)
-        tv[:, cols] = pv[:, cols] - dot3(sh, sl, xh[:, cols], xl[:, cols])
+    posterior_second()
 
     for rho in range(2):
         whole = w.at[pl.ds(0, NB[rho]), pl.ds(0, PIECE)]
@@ -477,6 +498,7 @@
             pltpu.VMEM((B, B), F32),
             pltpu.VMEM((B, B), F32),
             pltpu.VMEM((4, B, 128), F32),
+            pltpu.VMEM((2 * B, 128), F32),
             pltpu.VMEM((128, n), F32),
             dma((BLOCKS, 2)),
             dma((BLOCKS, 2)),

time: 65.9 us -> 64.8 us (0.983)
  Pallas kernels: 65 us -> 64 us
    pallas_call x1, Pallas kernels: 62.9 us -> 61.9 us  [local(): pl.pallas_call(kernel, out_shape=(pltpu.VMEM((n, n), F32), pltpu.VMEM((64...]
where the time goes in v5:
time: 64.8 us; the launch traced here: 64.7 us
  Pallas kernels  64 us (99%)
    pallas_call x1, Pallas kernels, local(): pl.pallas_call(kernel, out_shape=(pltpu.VMEM((n, n), F32), pltpu.VMEM((64...  61.9 us
    pallas_call x1, Pallas kernels, hand_on(): pl.pallas_call(hand_on_kernel, out_shape=(jax.ShapeDtypeStruct(current.sh...  2.13 us

profile of v5, /device:TPU:1, one launch (start us, length us, event | category | flops | bytes accessed | tf_op | source)
XLA Modules:
  0.0 64.7 jit_solution(1392993721698962351)
XLA Ops:
  0.6 61.9 %solve_update.1 = (f32[1024,1024]{1,0:T(8,128)S(1)}, f32[64,1024]{1,0:T(8,128)S(1)}) custom-call(f32[1024,1024]{1,0:T(8,128)} %c_hbm.1, f32[1024,1024]{1,0:T(8,128)} %f_hbm.1, f32[64,1024]{1,0:T(8,128)} %p_hbm.1), custom_call_target="tpu_custom_call" | custom-call | tf_op jit(solution)/shard_map/solve_update/pallas_call | solution.py:482
  62.5 2.1 %hand_on.1 = (f32[1024,1024]{1,0:T(8,128)}, f32[64,1024]{1,0:T(8,128)}) custom-call(f32[1024,1024]{1,0:T(8,128)S(1)} %get-tuple-element.4.a_in, f32[64,1024]{1,0:T(8,128)S(1)} %get-tuple-element.5.b_in), custom_call_target="tpu_custom_call" | custom-call | tf_op jit(solution)/shard_map/hand_on/pallas_call | solution.py:539

commit v6 on v5

--- a/solution.py
+++ b/solution.py
@@ -381,14 +381,6 @@
                         def _(act=act, rho=rho, il=il, n=n):
                             act(rho, il, n)
 
-        for rho in range(2):
-            for il in range(2):
-                inside, n = blocks_at(rho, u - LAG * depth[rho][il] - x_lag)[0]
-
-                @pl.when(inside)
-                def _(rho=rho, il=il, n=n):
-                    x_arrive(rho, il, n)
-
         @pl.when(u == 0)
         def _():
             load_f.wait()
@@ -425,6 +417,14 @@
         @pl.when(g == 12)
         def _():
             posterior_first()
+
+        for rho in range(2):
+            for il in range(2):
+                inside, n = blocks_at(rho, u - LAG * depth[rho][il] - x_lag)[0]
+
+                @pl.when(inside)
+                def _(rho=rho, il=il, n=n):
+                    x_arrive(rho, il, n)
 
         return carry
 

time: 64.8 us -> 65 us (level)
  no operation moved by 1% of the time
where the time goes in v6:
time: 65 us; the launch traced here: 64.9 us
  Pallas kernels  64.2 us (99%)
    pallas_call x1, Pallas kernels, local(): pl.pallas_call(kernel, out_shape=(pltpu.VMEM((n, n), F32), pltpu.VMEM((64...  62.1 us
    pallas_call x1, Pallas kernels, hand_on(): pl.pallas_call(hand_on_kernel, out_shape=(jax.ShapeDtypeStruct(current.sh...  2.13 us

profile of v6, /device:TPU:1, one launch (start us, length us, event | category | flops | bytes accessed | tf_op | source)
XLA Modules:
  0.0 64.9 jit_solution(3933347520733682329)
XLA Ops:
  0.6 62.1 %solve_update.1 = (f32[1024,1024]{1,0:T(8,128)S(1)}, f32[64,1024]{1,0:T(8,128)S(1)}) custom-call(f32[1024,1024]{1,0:T(8,128)} %c_hbm.1, f32[1024,1024]{1,0:T(8,128)} %f_hbm.1, f32[64,1024]{1,0:T(8,128)} %p_hbm.1), custom_call_target="tpu_custom_call" | custom-call | tf_op jit(solution)/shard_map/solve_update/pallas_call | solution.py:482
  62.8 2.1 %hand_on.1 = (f32[1024,1024]{1,0:T(8,128)}, f32[64,1024]{1,0:T(8,128)}) custom-call(f32[1024,1024]{1,0:T(8,128)S(1)} %get-tuple-element.4.a_in, f32[64,1024]{1,0:T(8,128)S(1)} %get-tuple-element.5.b_in), custom_call_target="tpu_custom_call" | custom-call | tf_op jit(solution)/shard_map/hand_on/pallas_call | solution.py:539
